TPU v7x, 32 devices: a whole 2x2x4 slice. The times are simulated.
32 devices in a mesh: pts: 16 (over z, y, x), rep: 2 (over core).
Axes of the slice: x: 2, y: 2, z: 4, core: 2. Of those that a mesh axis runs over, the one named last changes fastest.
Arguments:
- points: float32 [3, 65536], P(None, ('pts', 'rep')), may hold values from 0 to 1
- scales: float32 [3], replicated, may hold values from 0.1 to 0.3
- pivots: int32 [4, 128], replicated, may hold values from 0 to 65535, as said below
Outputs:
- factor: float32 [512, 65536], P(None, ('pts', 'rep'))
Inputs may be any that keep to these rules, and one draw needn't show every extreme that they name: All 512 indices are distinct. Point i lies on the device whose flat index over pts+rep is i // 2048; no device holds more than 16 pivots of one round, and some device holds exactly 16 in every round.
All inputs are finite; a program needn't handle non-finite values.
Results may differ from a plain program's by a relative error of at most 0.0003.
Values sent between devices are 32-bit elements; how exact they have to be, the bound alone decides.
A program may use at most 64 MiB of HBM per device.

v0:
```python
import functools
import math

import jax
import jax.numpy as jnp
from jax import lax
from jax.experimental import pallas as pl
from jax.experimental.pallas import tpu as pltpu
from jax.sharding import PartitionSpec as P

nugget_level = 0.1
HIGHEST = lax.Precision.HIGHEST
LANES = 128
GROUP = 8


def split_three(value):
    high = value.astype(jnp.bfloat16)
    rest = value - high.astype(jnp.float32)
    middle = rest.astype(jnp.bfloat16)
    low = (rest - middle.astype(jnp.float32)).astype(jnp.bfloat16)
    return high, middle, low


def exchange_kernel(
    mesh_shape, points_ref, pivots_ref, out_ref, table, mine, landed, send_sem, recv_sem
):
    pts_count, rep_count = mesh_shape
    devices = pts_count * rep_count
    here = lax.axis_index("pts") * rep_count + lax.axis_index("rep")
    dims, point_count = points_ref.shape
    rounds, pivot_count = pivots_ref.shape

    def place(step):
        peer = lax.rem(here + step, devices)
        return {"pts": peer // rep_count, "rep": lax.rem(peer, rep_count)}, peer

    barrier = pltpu.get_barrier_semaphore()

    def greet(step, carry):
        target, _ = place(step)
        pl.semaphore_signal(
            barrier, inc=1, device_id=target, device_id_type=pl.DeviceIdType.MESH
        )
        return carry

    lax.fori_loop(1, devices, greet, 0)

    chunks = point_count // LANES
    table[...] = jnp.zeros_like(table)
    for chunk in range(chunks):
        table[chunk * GROUP:chunk * GROUP + dims, :] = points_ref[
            :, chunk * LANES:(chunk + 1) * LANES
        ]
    pieces = split_three(table[...])
    lane_of = lax.broadcasted_iota(jnp.int32, (LANES, pivot_count), 0)
    for round_index in range(rounds):
        local = pivots_ref[round_index:round_index + 1, :] - here * point_count
        owned = (local >= 0) & (local < point_count)
        local = jnp.where(owned, local, 0)
        low = lax.rem(local, LANES)
        high = jnp.where(owned, local // LANES, -1)
        picks = (lane_of == low).astype(jnp.bfloat16)
        found = sum(
            jnp.dot(piece, picks, preferred_element_type=jnp.float32) for piece in pieces
        )
        total = jnp.zeros((GROUP, pivot_count), jnp.float32)
        for chunk in range(chunks):
            total = total + jnp.where(
                high == chunk, found[chunk * GROUP:(chunk + 1) * GROUP, :], 0.0
            )
        mine[:, round_index * pivot_count:(round_index + 1) * pivot_count] = total[:dims]

    pl.semaphore_wait(barrier, devices - 1)

    def copy_to(step):
        target, peer = place(step)
        return pltpu.make_async_remote_copy(
            src_ref=mine,
            dst_ref=landed.at[here],
            send_sem=send_sem.at[peer],
            recv_sem=recv_sem.at[here],
            device_id=target,
            device_id_type=pl.DeviceIdType.MESH,
        )

    def copy_from(step):
        _, peer = place(step)
        return pltpu.make_async_remote_copy(
            src_ref=mine,
            dst_ref=landed.at[peer],
            send_sem=send_sem.at[peer],
            recv_sem=recv_sem.at[peer],
            device_id=place(step)[0],
            device_id_type=pl.DeviceIdType.MESH,
        )

    def send(step, carry):
        copy_to(step).start()
        return carry

    def receive(step, total):
        copy_from(step).wait_recv()
        return total + landed[place(step)[1]]

    def finish(step, carry):
        copy_from(step).wait_send()
        return carry

    lax.fori_loop(1, devices, send, 0)
    total = lax.fori_loop(1, devices, receive, mine[...])
    out_ref[...] = jnp.zeros_like(out_ref)
    out_ref[:dims, :] = total
    lax.fori_loop(1, devices, finish, 0)


def reciprocal(value):
    rough = pl.reciprocal(value, approx=True)
    rough = rough * (2.0 - value * rough)
    return rough * (2.0 - value * rough)


def spread_lane(block, lane):
    return jnp.broadcast_to(block[:, lane:lane + 1], block.shape)


def spread_row(block, row):
    return jnp.broadcast_to(block[row:row + 1, :], block.shape)


def invert_factor(block):
    size = block.shape[0]
    count = size // GROUP
    row_of = lax.broadcasted_iota(jnp.int32, (GROUP, size), 0)
    lane_of = lax.broadcasted_iota(jnp.int32, (GROUP, size), 1)
    left = [block[GROUP * index:GROUP * (index + 1), :] for index in range(count)]
    right = [
        jnp.where(row_of + GROUP * index == lane_of, 1.0, 0.0) for index in range(count)
    ]
    result = []
    for panel in range(count):
        base = GROUP * panel
        spread = [spread_lane(left[panel], base + column) for column in range(GROUP)]
        s = {
            (i, j): spread_row(spread[j], i) for j in range(GROUP) for i in range(j, GROUP)
        }
        y_left = [spread_row(left[panel], row) for row in range(GROUP)]
        y_right = [spread_row(right[panel], row) for row in range(GROUP)]
        inverse = [None] * GROUP
        factor = {}
        for first in range(0, GROUP, 2):
            second = first + 1
            a, b, c = s[first, first], s[second, first], s[second, second]
            det = a * c - b * b
            inverse[first] = reciprocal(a)
            inverse[second] = a * reciprocal(det)
            for column in (first, second):
                for i in range(column + 1, GROUP):
                    factor[i, column] = s[i, column] * inverse[column]
                for j in range(column + 1, GROUP):
                    for i in range(j, GROUP):
                        if (i, j) == (second, second):
                            continue
                        s[i, j] = s[i, j] - factor[j, column] * s[i, column]
                for i in range(column + 1, GROUP):
                    y_left[i] = y_left[i] - factor[i, column] * y_left[column]
                    y_right[i] = y_right[i] - factor[i, column] * y_right[column]
        rows = jnp.zeros((GROUP, size), jnp.float32)
        roots = jnp.zeros((GROUP, size), jnp.float32)
        for row in range(GROUP):
            rows = jnp.where(row_of == row, y_right[row], rows)
            roots = jnp.where(row_of == row, inverse[row], roots)
        result.append(rows * jnp.sqrt(roots))
        if panel == count - 1:
            break
        w_left = [y_left[row] * inverse[row] for row in range(GROUP)]
        w_right = [y_right[row] * inverse[row] for row in range(GROUP)]
        for column in reversed(range(GROUP)):
            for row in range(column):
                w_left[row] = w_left[row] - factor[column, row] * w_left[column]
                w_right[row] = w_right[row] - factor[column, row] * w_right[column]
        for later in range(panel + 1, count):
            weights = [spread_lane(left[later], base + column) for column in range(GROUP)]
            for column in range(GROUP):
                left[later] = left[later] - weights[column] * w_left[column]
                right[later] = right[later] - weights[column] * w_right[column]
    return jnp.concatenate(result, axis=0)


def factor_kernel(
    rounds, points_ref, scales_ref, anchors_ref, out_ref, table, anchor_wide, rows_ref, held, sems
):
    dims, point_count = points_ref.shape
    total = anchors_ref.shape[1]
    pivot_count = total // rounds
    tile = 512
    tiles = point_count // tile
    constant = math.sqrt(0.5 * math.log2(math.e))
    weights = [
        constant / jnp.full((1, LANES), scales_ref[axis], jnp.float32) for axis in range(dims)
    ]
    upright = jnp.transpose(anchors_ref[...])
    for axis in range(dims):
        anchor_wide[axis] = upright[:, axis:axis + 1] * weights[axis]
        rows_ref[axis:axis + 1, :] = anchors_ref[axis:axis + 1, :] * jnp.concatenate(
            [weights[axis]] * (total // LANES), axis=1
        )

    def covariance(start, count, targets):
        pieces = []
        for column in range(targets[0].shape[1] // LANES):
            squared = None
            for axis in range(dims):
                offset = anchor_wide[axis, pl.ds(start, count), :] - targets[axis][
                    :, column * LANES:(column + 1) * LANES
                ]
                square = offset * offset
                squared = square if squared is None else squared + square
            pieces.append(jnp.exp2(-squared))
        return jnp.concatenate(pieces, axis=1)

    def one_round(round_index, carry):
        start = pl.multiple_of(round_index * pivot_count, pivot_count)
        here = pl.ds(start, pivot_count)
        unit = jnp.where(
            lax.broadcasted_iota(jnp.int32, (pivot_count, total), 0) + start
            == lax.broadcasted_iota(jnp.int32, (pivot_count, total), 1),
            1.0,
            0.0,
        )
        own = covariance(
            start, pivot_count, [rows_ref[axis:axis + 1, :] for axis in range(dims)]
        )
        table[here, :] = jnp.concatenate([own + nugget_level * unit, unit], axis=1)

        def subtract(earlier, inner):
            seen = pl.ds(pl.multiple_of(earlier * pivot_count, pivot_count), pivot_count)
            table[here, :] = table[here, :] - lax.dot_general(
                table[seen, here],
                table[seen, :],
                (((0,), (0,)), ((), ())),
                precision=HIGHEST,
                preferred_element_type=jnp.float32,
            )
            return inner

        lax.fori_loop(0, round_index, subtract, 0)
        inverse = invert_factor(table[here, here])
        table[here, :] = jnp.dot(
            inverse, table[here, :], precision=HIGHEST, preferred_element_type=jnp.float32
        )
        return carry

    lax.fori_loop(0, rounds, one_round, 0)

    def copy_out(index):
        span = pl.ds(pl.multiple_of(index * tile, tile), tile)
        return pltpu.make_async_copy(held.at[:, span], out_ref.at[:, span], sems.at[index])

    def one_tile(index, carry):
        span = pl.ds(pl.multiple_of(index * tile, tile), tile)
        targets = [
            points_ref[axis:axis + 1, span]
            * jnp.concatenate([weights[axis]] * (tile // LANES), axis=1)
            for axis in range(dims)
        ]
        block = covariance(0, total, targets)
        for round_index in range(rounds):
            low, high = round_index * pivot_count, (round_index + 1) * pivot_count
            held[low:high, span] = jnp.dot(
                table[low:high, total:total + high],
                block[:high],
                precision=HIGHEST,
                preferred_element_type=jnp.float32,
            )
        copy_out(index).start()
        return carry

    lax.fori_loop(0, tiles, one_tile, 0)

    def finish(index, carry):
        copy_out(index).wait()
        return carry

    lax.fori_loop(0, tiles, finish, 0)


def per_device(mesh_shape, points, scales, pivots):
    dims, point_count = points.shape
    rounds, pivot_count = pivots.shape
    total = rounds * pivot_count
    devices = mesh_shape[0] * mesh_shape[1]
    vmem = pl.BlockSpec(memory_space=pltpu.VMEM)
    anchors = pl.pallas_call(
        functools.partial(exchange_kernel, mesh_shape),
        out_shape=jax.ShapeDtypeStruct((GROUP, total), jnp.float32),
        in_specs=[vmem, vmem],
        out_specs=vmem,
        scratch_shapes=[
            pltpu.VMEM((point_count // LANES * GROUP, LANES), jnp.float32),
            pltpu.VMEM((dims, total), jnp.float32),
            pltpu.VMEM((devices, dims, total), jnp.float32),
            pltpu.SemaphoreType.DMA((devices,)),
            pltpu.SemaphoreType.DMA((devices,)),
        ],
        compiler_params=pltpu.CompilerParams(
            collective_id=0, has_side_effects=True, vmem_limit_bytes=32 * 2 ** 20
        ),
        name="exchange_anchors",
    )(points, pivots)
    return pl.pallas_call(
        functools.partial(factor_kernel, rounds),
        out_shape=jax.ShapeDtypeStruct((total, point_count), jnp.float32),
        in_specs=[vmem, pl.BlockSpec(memory_space=pltpu.SMEM), vmem],
        out_specs=pl.BlockSpec(memory_space=pl.ANY),
        scratch_shapes=[
            pltpu.VMEM((total, 2 * total), jnp.float32),
            pltpu.VMEM((dims, total, LANES), jnp.float32),
            pltpu.VMEM((GROUP, total), jnp.float32),
            pltpu.VMEM((total, point_count), jnp.float32),
            pltpu.SemaphoreType.DMA((point_count // 512,)),
        ],
        compiler_params=pltpu.CompilerParams(vmem_limit_bytes=48 * 2 ** 20),
        name="factor_columns",
    )(points, scales, anchors)


def solution(mesh):
    placed = (P(None, ("pts", "rep")), P(), P())
    mesh_shape = (mesh.shape["pts"], mesh.shape["rep"])
    return jax.shard_map(
        functools.partial(per_device, mesh_shape),
        mesh=mesh,
        in_specs=placed,
        out_specs=P(None, ("pts", "rep")),
        check_vma=False,
    )
```

profile of v0, /device:TPU:0, one launch (start us, length us, event | category | flops | bytes accessed | tf_op | source)
XLA Modules:
  0.0 50.6 jit_solution(11866144723409910593)
XLA Ops:
  0.0 0.0 copy-start
  0.0 0.8 %copy-done = f32[3,2048]{1,0:T(4,128)S(1)} copy-done((f32[3,2048]{1,0:T(4,128)S(1)}, f32[3,2048]{1,0:T(4,128)}, u32[]{:S(2)}) %copy-start) | copy-done | bytes 24600
  0.8 0.0 copy-start.2
  0.8 0.7 %copy-done.2 = s32[4,128]{1,0:T(4,128)S(1)} copy-done((s32[4,128]{1,0:T(4,128)S(1)}, s32[4,128]{1,0:T(4,128)}, u32[]{:S(2)}) %copy-start.2) | copy-done | bytes 2072
  1.4 12.6 %exchange_anchors.1.anchors_ref = f32[8,512]{1,0:T(8,128)S(1)} custom-call(f32[3,2048]{1,0:T(4,128)S(1)} %copy-done, s32[4,128]{1,0:T(4,128)S(1)} %copy-done.2), custom_call_target="tpu_custom_call" | custom-call | tf_op jit(solution)/shard_map/exchange_anchors/pallas_call | solution.py:294
  14.1 0.0 copy-start.1
  14.1 0.7 %copy-done.1 = f32[3,2048]{1,0:T(4,128)S(1)} copy-done((f32[3,2048]{1,0:T(4,128)S(1)}, f32[3,2048]{1,0:T(4,128)}, u32[]{:S(2)}) %copy-start.1) | copy-done | bytes 24600
  14.8 0.0 copy-start.3
  14.8 0.7 %copy-done.3 = f32[3]{0:T(128)S(1)} copy-done((f32[3]{0:T(128)S(1)}, f32[3]{0:T(128)}, u32[]{:S(2)}) %copy-start.3) | copy-done | bytes 36
  15.5 35.1 %factor_columns.1 = f32[512,2048]{1,0:T(8,128)} custom-call(f32[3,2048]{1,0:T(4,128)S(1)} %copy-done.1, f32[3]{0:T(128)S(1)} %copy-done.3, f32[8,512]{1,0:T(8,128)S(1)} %exchange_anchors.1.anchors_ref), custom_call_target="tpu_custom_call" | custom-call | tf_op jit(solution)/shard_map/factor_columns/pallas_call | solution.py:311
Async XLA Ops:
  0.0 0.8 %copy-start = (f32[3,2048]{1,0:T(4,128)S(1)}, f32[3,2048]{1,0:T(4,128)}, u32[]{:S(2)}) copy-start(f32[3,2048]{1,0:T(4,128)} %points_ref.3) | copy-start | bytes 73732
  0.8 0.7 %copy-start.2 = (s32[4,128]{1,0:T(4,128)S(1)}, s32[4,128]{1,0:T(4,128)}, u32[]{:S(2)}) copy-start(s32[4,128]{1,0:T(4,128)} %pivots_ref.1) | copy-start | bytes 6148
  14.1 0.8 %copy-start.1 = (f32[3,2048]{1,0:T(4,128)S(1)}, f32[3,2048]{1,0:T(4,128)}, u32[]{:S(2)}) copy-start(f32[3,2048]{1,0:T(4,128)} %points_ref.3) | copy-start | bytes 73732
  14.8 0.7 %copy-start.3 = (f32[3]{0:T(128)S(1)}, f32[3]{0:T(128)}, u32[]{:S(2)}) copy-start(f32[3]{0:T(128)} %scales_ref.1) | copy-start | bytes 40
where the time goes:
time: 51.2 us; the launch traced here: 50.6 us
  Pallas kernels  47.7 us (93%)
  local copies, waits for them, and re-layouts  2.85 us (6%)
    pallas_call x1, Pallas kernels, per_device(): pl.pallas_call(functools.partial(factor_kernel, rounds), out_shape=jax.Sh...  35.1 us
    pallas_call x1, Pallas kernels, per_device(): pl.pallas_call(functools.partial(exchange_kernel, mesh_shape), out_shape=...  12.6 us
    unnamed x8, local copies, waits for them, and re-layouts  2.85 us

commit v1 on v0

v1 whole, which is shorter than its diff:
```python
import functools
import math

import jax
import jax.numpy as jnp
from jax import lax
from jax.experimental import pallas as pl
from jax.experimental.pallas import tpu as pltpu
from jax.sharding import PartitionSpec as P

nugget_level = 0.1
HIGHEST = lax.Precision.HIGHEST
LANES = 128
GROUP = 8


def split_three(value):
    high = value.astype(jnp.bfloat16)
    rest = value - high.astype(jnp.float32)
    middle = rest.astype(jnp.bfloat16)
    low = (rest - middle.astype(jnp.float32)).astype(jnp.bfloat16)
    return high, middle, low


def exchange_kernel(
    mesh_shape,
    inner,
    points_hbm,
    scales_hbm,
    pivots_hbm,
    out_ref,
    points_ref,
    scales_ref,
    pivots_ref,
    table,
    mine,
    pair_sum,
    landed_near,
    landed_far,
    load_sems,
    near_send,
    near_recv,
    far_send,
    far_recv,
):
    pts_count, rep_count = mesh_shape
    devices = pts_count * rep_count
    here = lax.axis_index("pts") * rep_count + lax.axis_index("rep")
    dims, point_count = points_ref.shape
    rounds, pivot_count = pivots_ref.shape
    within = lax.rem(here, inner)

    def place(peer):
        return {"pts": peer // rep_count, "rep": lax.rem(peer, rep_count)}

    near = [place(here - within + lax.rem(within + step, inner)) for step in range(1, inner)]
    far = [place(lax.rem(here + step * inner, devices)) for step in range(1, devices // inner)]

    loads = [
        pltpu.make_async_copy(points_hbm, points_ref, load_sems.at[0]),
        pltpu.make_async_copy(pivots_hbm, pivots_ref, load_sems.at[1]),
        pltpu.make_async_copy(scales_hbm, scales_ref, load_sems.at[2]),
    ]
    for load in loads:
        load.start()

    barrier = pltpu.get_barrier_semaphore()
    for target in near + far:
        pl.semaphore_signal(
            barrier, inc=1, device_id=target, device_id_type=pl.DeviceIdType.MESH
        )

    chunks = point_count // LANES
    table[...] = jnp.zeros_like(table)
    for load in loads:
        load.wait()
    for chunk in range(chunks):
        table[chunk * GROUP:chunk * GROUP + dims, :] = points_ref[
            :, chunk * LANES:(chunk + 1) * LANES
        ]
    pieces = split_three(table[...])
    lane_of = lax.broadcasted_iota(jnp.int32, (LANES, pivot_count), 0)
    for round_index in range(rounds):
        local = pivots_ref[round_index:round_index + 1, :] - here * point_count
        owned = (local >= 0) & (local < point_count)
        local = jnp.where(owned, local, 0)
        low = lax.rem(local, LANES)
        high = jnp.where(owned, local // LANES, -1)
        picks = (lane_of == low).astype(jnp.bfloat16)
        found = sum(
            jnp.dot(piece, picks, preferred_element_type=jnp.float32) for piece in pieces
        )
        total = jnp.zeros((GROUP, pivot_count), jnp.float32)
        for chunk in range(chunks):
            total = total + jnp.where(
                high == chunk, found[chunk * GROUP:(chunk + 1) * GROUP, :], 0.0
            )
        mine[:, round_index * pivot_count:(round_index + 1) * pivot_count] = total[:dims]

    pl.semaphore_wait(barrier, len(near) + len(far))

    def exchange(source, landed, targets, send_sems, recv_sems):
        copies = [
            pltpu.make_async_remote_copy(
                src_ref=source,
                dst_ref=landed.at[index],
                send_sem=send_sems.at[index],
                recv_sem=recv_sems.at[index],
                device_id=target,
                device_id_type=pl.DeviceIdType.MESH,
            )
            for index, target in enumerate(targets)
        ]
        for copy in copies:
            copy.start()
        total = source[...]
        for index, copy in enumerate(copies):
            copy.wait_recv()
            total = total + landed[index]
        return total, copies

    total, near_copies = exchange(mine, landed_near, near, near_send, near_recv)
    pair_sum[...] = total
    total, far_copies = exchange(pair_sum, landed_far, far, far_send, far_recv)
    constant = math.sqrt(0.5 * math.log2(math.e))
    out_ref[...] = jnp.zeros_like(out_ref)
    for axis in range(dims):
        weight = constant / jnp.full((1, total.shape[1]), scales_ref[axis], jnp.float32)
        out_ref[axis:axis + 1, :] = total[axis:axis + 1, :] * weight
        out_ref[dims + axis:dims + axis + 1, :] = weight
    for copy in near_copies + far_copies:
        copy.wait_send()


def reciprocal(value):
    return pl.reciprocal(value, approx=True)


def spread_lane(block, lane):
    return jnp.broadcast_to(block[:, lane:lane + 1], block.shape)


def spread_row(block, row):
    return jnp.broadcast_to(block[row:row + 1, :], block.shape)


def invert_factor(block, beside):
    size = block.shape[0]
    count = size // GROUP
    row_of = lax.broadcasted_iota(jnp.int32, (GROUP, size), 0)
    lane_of = lax.broadcasted_iota(jnp.int32, (GROUP, size), 1)
    left = [block[GROUP * index:GROUP * (index + 1), :] for index in range(count)]
    right = [
        jnp.where(row_of + GROUP * index == lane_of, 1.0, 0.0) for index in range(count)
    ]
    result = []
    for panel in range(count):
        base = GROUP * panel
        beside(panel, count)
        spread = [spread_lane(left[panel], base + column) for column in range(GROUP)]
        s = {
            (i, j): spread_row(spread[j], i) for j in range(GROUP) for i in range(j, GROUP)
        }
        y_left = [spread_row(left[panel], row) for row in range(GROUP)]
        y_right = [spread_row(right[panel], row) for row in range(GROUP)]
        inverse = [None] * GROUP
        factor = {}
        for first in range(0, GROUP, 2):
            second = first + 1
            a, b, c = s[first, first], s[second, first], s[second, second]
            det = a * c - b * b
            inverse[first] = reciprocal(a)
            inverse[second] = a * reciprocal(det)
            for column in (first, second):
                for i in range(column + 1, GROUP):
                    factor[i, column] = s[i, column] * inverse[column]
                for j in range(column + 1, GROUP):
                    for i in range(j, GROUP):
                        if (i, j) == (second, second):
                            continue
                        s[i, j] = s[i, j] - factor[j, column] * s[i, column]
                for i in range(column + 1, GROUP):
                    y_left[i] = y_left[i] - factor[i, column] * y_left[column]
                    y_right[i] = y_right[i] - factor[i, column] * y_right[column]
        rows = jnp.zeros((GROUP, size), jnp.float32)
        roots = jnp.zeros((GROUP, size), jnp.float32)
        for row in range(GROUP):
            rows = jnp.where(row_of == row, y_right[row], rows)
            roots = jnp.where(row_of == row, inverse[row], roots)
        result.append(rows * jnp.sqrt(roots))
        if panel == count - 1:
            break
        w_left = [y_left[row] * inverse[row] for row in range(GROUP)]
        w_right = [y_right[row] * inverse[row] for row in range(GROUP)]
        for column in reversed(range(GROUP)):
            for row in range(column):
                w_left[row] = w_left[row] - factor[column, row] * w_left[column]
                w_right[row] = w_right[row] - factor[column, row] * w_right[column]
        for later in range(panel + 1, count):
            weights = [spread_lane(left[later], base + column) for column in range(GROUP)]
            for column in range(GROUP):
                left[later] = left[later] - weights[column] * w_left[column]
                right[later] = right[later] - weights[column] * w_right[column]
    return jnp.concatenate(result, axis=0)


def factor_kernel(
    rounds,
    points_hbm,
    anchors_ref,
    out_ref,
    points_ref,
    table,
    anchor_wide,
    inverse_high,
    inverse_low,
    block_high,
    block_low,
    held,
    load_sem,
    sems,
):
    dims, point_count = points_ref.shape
    total = anchors_ref.shape[1]
    pivot_count = total // rounds
    tile = point_count // rounds
    load = pltpu.make_async_copy(points_hbm, points_ref, load_sem)
    load.start()
    weights = [anchors_ref[dims + axis:dims + axis + 1, :LANES] for axis in range(dims)]
    upright = jnp.transpose(anchors_ref[...])
    for axis in range(dims):
        anchor_wide[axis] = jnp.broadcast_to(upright[:, axis:axis + 1], (total, LANES))
    load.wait()

    def covariance(start, count, targets):
        pieces = []
        for column in range(targets[0].shape[1] // LANES):
            squared = None
            for axis in range(dims):
                offset = anchor_wide[axis, pl.ds(start, count), :] - targets[axis][
                    :, column * LANES:(column + 1) * LANES
                ]
                square = offset * offset
                squared = square if squared is None else squared + square
            pieces.append(jnp.exp2(-squared))
        return jnp.concatenate(pieces, axis=1)

    def one_round(round_index, carry):
        start = pl.multiple_of(round_index * pivot_count, pivot_count)
        here = pl.ds(start, pivot_count)
        span = pl.ds(pl.multiple_of(round_index * tile, tile), tile)
        lane_of = lax.broadcasted_iota(jnp.int32, (pivot_count, total), 1)
        row_of = lax.broadcasted_iota(jnp.int32, (pivot_count, total), 0) + start
        own = covariance(
            start, pivot_count, [anchors_ref[axis:axis + 1, :] for axis in range(dims)]
        )
        own = own + jnp.where(row_of == lane_of, nugget_level, 0.0)
        table[here, :] = jnp.where(lane_of >= start, own, 0.0)

        def subtract(earlier, inner):
            before = pl.multiple_of(earlier * pivot_count, pivot_count)
            seen = pl.ds(before, pivot_count)
            kept = (lane_of < before + pivot_count) | (lane_of >= start)
            table[here, :] = table[here, :] - lax.dot_general(
                table[seen, here],
                jnp.where(kept, table[seen, :], 0.0),
                (((0,), (0,)), ((), ())),
                precision=HIGHEST,
                preferred_element_type=jnp.float32,
            )
            return inner

        lax.fori_loop(0, round_index, subtract, 0)

        targets = [
            points_ref[axis:axis + 1, span]
            * jnp.concatenate([weights[axis]] * (tile // LANES), axis=1)
            for axis in range(dims)
        ]

        def beside(step, steps):
            size = total // steps
            part = slice(step * size, (step + 1) * size)
            values = covariance(step * size, size, targets)
            high = values.astype(jnp.bfloat16)
            block_high[part, span] = high
            block_low[part, span] = (values - high.astype(jnp.float32)).astype(jnp.bfloat16)

        inverse = invert_factor(table[here, here], beside)
        table[here, :] = jnp.dot(
            inverse, table[here, :], precision=HIGHEST, preferred_element_type=jnp.float32
        )
        table[here, here] = inverse
        final = jnp.where(lane_of < start + pivot_count, table[here, :], 0.0)
        high = final.astype(jnp.bfloat16)
        inverse_high[here, :] = high
        inverse_low[here, :] = (final - high.astype(jnp.float32)).astype(jnp.bfloat16)
        return carry

    lax.fori_loop(0, rounds, one_round, 0)

    half = total // 2

    def copy_out(index):
        span = pl.ds(pl.multiple_of(index * tile, tile), tile)
        return pltpu.make_async_copy(held.at[:, span], out_ref.at[:, span], sems.at[index])

    def product(rows, depth, span):
        def multiply(a, b):
            return jnp.dot(
                a[rows, depth], b[depth, span], preferred_element_type=jnp.float32
            )

        return (
            multiply(inverse_high, block_low) + multiply(inverse_low, block_high)
        ) + multiply(inverse_high, block_high)

    def one_tile(index, carry):
        span = pl.ds(pl.multiple_of(index * tile, tile), tile)
        top, bottom = slice(0, half), slice(half, total)
        held[:, span] = product(slice(0, total), top, span)
        held[bottom, span] = held[bottom, span] + product(bottom, bottom, span)
        copy_out(index).start()
        return carry

    lax.fori_loop(0, rounds, one_tile, 0)

    def finish(index, carry):
        copy_out(index).wait()
        return carry

    lax.fori_loop(0, rounds, finish, 0)


def per_device(mesh_shape, points, scales, pivots):
    dims, point_count = points.shape
    rounds, pivot_count = pivots.shape
    total = rounds * pivot_count
    devices = mesh_shape[0] * mesh_shape[1]
    inner = 1
    while inner * inner < devices:
        inner *= 2
    if devices % inner:
        inner = devices
    near, far = inner - 1, devices // inner - 1
    vmem = pl.BlockSpec(memory_space=pltpu.VMEM)
    anywhere = pl.BlockSpec(memory_space=pl.ANY)
    anchors = pl.pallas_call(
        functools.partial(exchange_kernel, mesh_shape, inner),
        out_shape=jax.ShapeDtypeStruct((GROUP, total), jnp.float32),
        in_specs=[anywhere] * 3,
        out_specs=vmem,
        scratch_shapes=[
            pltpu.VMEM((dims, point_count), jnp.float32),
            pltpu.SMEM((dims,), jnp.float32),
            pltpu.VMEM((rounds, pivot_count), jnp.int32),
            pltpu.VMEM((point_count // LANES * GROUP, LANES), jnp.float32),
            pltpu.VMEM((dims, total), jnp.float32),
            pltpu.VMEM((dims, total), jnp.float32),
            pltpu.VMEM((max(near, 1), dims, total), jnp.float32),
            pltpu.VMEM((max(far, 1), dims, total), jnp.float32),
            pltpu.SemaphoreType.DMA((3,)),
            pltpu.SemaphoreType.DMA((max(near, 1),)),
            pltpu.SemaphoreType.DMA((max(near, 1),)),
            pltpu.SemaphoreType.DMA((max(far, 1),)),
            pltpu.SemaphoreType.DMA((max(far, 1),)),
        ],
        compiler_params=pltpu.CompilerParams(
            collective_id=0, has_side_effects=True, vmem_limit_bytes=56 * 2 ** 20
        ),
        name="exchange_anchors",
    )(points, scales, pivots)
    return pl.pallas_call(
        functools.partial(factor_kernel, rounds),
        out_shape=jax.ShapeDtypeStruct((total, point_count), jnp.float32),
        in_specs=[anywhere, vmem],
        out_specs=anywhere,
        scratch_shapes=[
            pltpu.VMEM((dims, point_count), jnp.float32),
            pltpu.VMEM((total, total), jnp.float32),
            pltpu.VMEM((dims, total, LANES), jnp.float32),
            pltpu.VMEM((total, total), jnp.bfloat16),
            pltpu.VMEM((total, total), jnp.bfloat16),
            pltpu.VMEM((total, point_count), jnp.bfloat16),
            pltpu.VMEM((total, point_count), jnp.bfloat16),
            pltpu.VMEM((total, point_count), jnp.float32),
            pltpu.SemaphoreType.DMA,
            pltpu.SemaphoreType.DMA((rounds,)),
        ],
        compiler_params=pltpu.CompilerParams(vmem_limit_bytes=56 * 2 ** 20),
        name="factor_columns",
    )(points, anchors)


def solution(mesh):
    placed = (P(None, ("pts", "rep")), P(), P())
    mesh_shape = (mesh.shape["pts"], mesh.shape["rep"])
    return jax.shard_map(
        functools.partial(per_device, mesh_shape),
        mesh=mesh,
        in_specs=placed,
        out_specs=P(None, ("pts", "rep")),
        check_vma=False,
    )
```

time: 51.2 us -> 42.2 us (0.82)
  Pallas kernels: 47.7 us -> 41.9 us
  local copies, waits for them, and re-layouts: 2.85 us -> 0 us
    pallas_call x1, Pallas kernels: 35.1 us -> 29.2 us  [per_device(): pl.pallas_call(functools.partial(factor_kernel, rounds), out_shape=jax.Sh...]
    unnamed x8 -> x0, local copies, waits for them, and re-layouts: 2.85 us -> none
where the time goes in v1:
time: 42.2 us; the launch traced here: 41.9 us
  Pallas kernels  41.9 us (99%)
    pallas_call x1, Pallas kernels, per_device(): pl.pallas_call(functools.partial(factor_kernel, rounds), out_shape=jax.Sh...  29.2 us
    pallas_call x1, Pallas kernels, per_device(): pl.pallas_call(functools.partial(exchange_kernel, mesh_shape, inner), out...  12.7 us

profile of v1, /device:TPU:0, one launch (start us, length us, event | category | flops | bytes accessed | tf_op | source)
XLA Modules:
  0.0 41.9 jit_solution(8325832668836759888)
XLA Ops:
  0.0 12.7 %exchange_anchors.1.anchors_ref = f32[8,512]{1,0:T(8,128)} custom-call(f32[3,2048]{1,0:T(4,128)} %points_hbm.3, f32[3]{0:T(128)} %scales_hbm.1, s32[4,128]{1,0:T(4,128)} %pivots_hbm.1), custom_call_target="tpu_custom_call" | custom-call | tf_op jit(solution)/shard_map/exchange_anchors/pallas_call | solution.py:348
  12.7 29.2 %factor_columns.1 = f32[512,2048]{1,0:T(8,128)} custom-call(f32[3,2048]{1,0:T(4,128)} %points_hbm.3, f32[8,512]{1,0:T(8,128)} %exchange_anchors.1.anchors_ref), custom_call_target="tpu_custom_call" | custom-call | tf_op jit(solution)/shard_map/factor_columns/pallas_call | solution.py:373

commit v2 on v1

--- a/solution.py
+++ b/solution.py
@@ -149,28 +149,39 @@
     count = size // GROUP
     row_of = lax.broadcasted_iota(jnp.int32, (GROUP, size), 0)
     lane_of = lax.broadcasted_iota(jnp.int32, (GROUP, size), 1)
-    left = [block[GROUP * index:GROUP * (index + 1), :] for index in range(count)]
-    right = [
-        jnp.where(row_of + GROUP * index == lane_of, 1.0, 0.0) for index in range(count)
-    ]
+    state = [block[GROUP * index:GROUP * (index + 1), :] for index in range(count)]
     result = []
     for panel in range(count):
         base = GROUP * panel
         beside(panel, count)
-        spread = [spread_lane(left[panel], base + column) for column in range(GROUP)]
+        inside = (lane_of >= base) & (lane_of < base + GROUP)
+        unit = jnp.where(row_of + base == lane_of, 1.0, 0.0)
+        spread = [spread_lane(state[panel], base + column) for column in range(GROUP)]
         s = {
             (i, j): spread_row(spread[j], i) for j in range(GROUP) for i in range(j, GROUP)
         }
-        y_left = [spread_row(left[panel], row) for row in range(GROUP)]
-        y_right = [spread_row(right[panel], row) for row in range(GROUP)]
+        own = jnp.where(inside, unit, state[panel])
+        y = [spread_row(own, row) for row in range(GROUP)]
+        more = panel + 1 < count
+        if more:
+            beyond = [
+                spread_lane(state[panel + 1], base + column) for column in range(GROUP)
+            ]
+            follower = jnp.where(inside, 0.0, state[panel + 1])
         inverse = [None] * GROUP
         factor = {}
+        z = [None] * GROUP
         for first in range(0, GROUP, 2):
             second = first + 1
             a, b, c = s[first, first], s[second, first], s[second, second]
-            det = a * c - b * b
+            over = reciprocal(a * c - b * b)
             inverse[first] = reciprocal(a)
-            inverse[second] = a * reciprocal(det)
+            inverse[second] = a * over
+            urgent = {
+                (i, j)
+                for j in range(second + 1, min(second + 3, GROUP))
+                for i in range(j, min(second + 3, GROUP))
+            }
             for column in (first, second):
                 for i in range(column + 1, GROUP):
                     factor[i, column] = s[i, column] * inverse[column]
@@ -178,29 +189,38 @@
                     for i in range(j, GROUP):
                         if (i, j) == (second, second):
                             continue
-                        s[i, j] = s[i, j] - factor[j, column] * s[i, column]
+                        if column == second and (i, j) in urgent:
+                            change = (s[i, column] * s[j, column]) * a * over
+                        else:
+                            change = factor[j, column] * s[i, column]
+                        s[i, j] = s[i, j] - change
                 for i in range(column + 1, GROUP):
-                    y_left[i] = y_left[i] - factor[i, column] * y_left[column]
-                    y_right[i] = y_right[i] - factor[i, column] * y_right[column]
-        rows = jnp.zeros((GROUP, size), jnp.float32)
-        roots = jnp.zeros((GROUP, size), jnp.float32)
-        for row in range(GROUP):
-            rows = jnp.where(row_of == row, y_right[row], rows)
+                    y[i] = y[i] - factor[i, column] * y[column]
+                z[column] = y[column] * inverse[column]
+                if more:
+                    for k in range(column + 1, GROUP):
+                        beyond[k] = beyond[k] - beyond[column] * factor[k, column]
+                    follower = follower - beyond[column] * z[column]
+        rows, roots = y[0], inverse[0]
+        for row in range(1, GROUP):
+            rows = jnp.where(row_of == row, y[row], rows)
             roots = jnp.where(row_of == row, inverse[row], roots)
-        result.append(rows * jnp.sqrt(roots))
-        if panel == count - 1:
+        result.append(jnp.where(lane_of < base + GROUP, rows * jnp.sqrt(roots), 0.0))
+        if not more:
             break
-        w_left = [y_left[row] * inverse[row] for row in range(GROUP)]
-        w_right = [y_right[row] * inverse[row] for row in range(GROUP)]
+        state[panel + 1] = follower
+        if panel + 2 == count:
+            continue
         for column in reversed(range(GROUP)):
             for row in range(column):
-                w_left[row] = w_left[row] - factor[column, row] * w_left[column]
-                w_right[row] = w_right[row] - factor[column, row] * w_right[column]
-        for later in range(panel + 1, count):
-            weights = [spread_lane(left[later], base + column) for column in range(GROUP)]
-            for column in range(GROUP):
-                left[later] = left[later] - weights[column] * w_left[column]
-                right[later] = right[later] - weights[column] * w_right[column]
+                z[row] = z[row] - factor[column, row] * z[column]
+        for later in range(panel + 2, count):
+            terms = [
+                spread_lane(state[later], base + column) * z[column] for column in range(GROUP)
+            ]
+            while len(terms) > 1:
+                terms = [terms[at] + terms[at + 1] for at in range(0, len(terms), 2)]
+            state[later] = jnp.where(inside, 0.0, state[later]) - terms[0]
     return jnp.concatenate(result, axis=0)
 
 

time: 42.2 us -> 39 us (0.924)
  Pallas kernels: 41.9 us -> 38.7 us
    pallas_call x1, Pallas kernels: 29.2 us -> 26 us  [per_device(): pl.pallas_call(functools.partial(factor_kernel, rounds), out_shape=jax.Sh...]
where the time goes in v2:
time: 39 us; the launch traced here: 38.7 us
  Pallas kernels  38.7 us (99%)
    pallas_call x1, Pallas kernels, per_device(): pl.pallas_call(functools.partial(factor_kernel, rounds), out_shape=jax.Sh...  26 us
    pallas_call x1, Pallas kernels, per_device(): pl.pallas_call(functools.partial(exchange_kernel, mesh_shape, inner), out...  12.7 us

profile of v2, /device:TPU:0, one launch (start us, length us, event | category | flops | bytes accessed | tf_op | source)
XLA Modules:
  0.0 38.7 jit_solution(11329271323907632920)
XLA Ops:
  0.0 12.7 %exchange_anchors.1.anchors_ref = f32[8,512]{1,0:T(8,128)} custom-call(f32[3,2048]{1,0:T(4,128)} %points_hbm.3, f32[3]{0:T(128)} %scales_hbm.1, s32[4,128]{1,0:T(4,128)} %pivots_hbm.1), custom_call_target="tpu_custom_call" | custom-call | tf_op jit(solution)/shard_map/exchange_anchors/pallas_call | solution.py:368
  12.7 26.0 %factor_columns.1 = f32[512,2048]{1,0:T(8,128)} custom-call(f32[3,2048]{1,0:T(4,128)} %points_hbm.3, f32[8,512]{1,0:T(8,128)} %exchange_anchors.1.anchors_ref), custom_call_target="tpu_custom_call" | custom-call | tf_op jit(solution)/shard_map/factor_columns/pallas_call | solution.py:393

commit v3 on v2

--- a/solution.py
+++ b/solution.py
@@ -224,6 +224,19 @@
     return jnp.concatenate(result, axis=0)
 
 
+def split_two(value):
+    high = value.astype(jnp.bfloat16)
+    return high, (value - high.astype(jnp.float32)).astype(jnp.bfloat16)
+
+
+def product(a, b):
+    return jnp.dot(
+        jnp.concatenate([a[0], a[0], a[1]], axis=1),
+        jnp.concatenate([b[0], b[1], b[0]], axis=0),
+        preferred_element_type=jnp.float32,
+    )
+
+
 def factor_kernel(
     rounds,
     points_hbm,
@@ -232,10 +245,10 @@
     points_ref,
     table,
     anchor_wide,
-    inverse_high,
-    inverse_low,
-    block_high,
-    block_low,
+    rest_high,
+    rest_low,
+    done_high,
+    done_low,
     held,
     load_sem,
     sems,
@@ -243,7 +256,7 @@
     dims, point_count = points_ref.shape
     total = anchors_ref.shape[1]
     pivot_count = total // rounds
-    tile = point_count // rounds
+    chunk = 2 * LANES
     load = pltpu.make_async_copy(points_hbm, points_ref, load_sem)
     load.start()
     weights = [anchors_ref[dims + axis:dims + axis + 1, :LANES] for axis in range(dims)]
@@ -252,12 +265,12 @@
         anchor_wide[axis] = jnp.broadcast_to(upright[:, axis:axis + 1], (total, LANES))
     load.wait()
 
-    def covariance(start, count, targets):
+    def covariance(start, targets):
         pieces = []
         for column in range(targets[0].shape[1] // LANES):
             squared = None
             for axis in range(dims):
-                offset = anchor_wide[axis, pl.ds(start, count), :] - targets[axis][
+                offset = anchor_wide[axis, start:start + pivot_count, :] - targets[axis][
                     :, column * LANES:(column + 1) * LANES
                 ]
                 square = offset * offset
@@ -265,91 +278,81 @@
             pieces.append(jnp.exp2(-squared))
         return jnp.concatenate(pieces, axis=1)
 
-    def one_round(round_index, carry):
-        start = pl.multiple_of(round_index * pivot_count, pivot_count)
-        here = pl.ds(start, pivot_count)
-        span = pl.ds(pl.multiple_of(round_index * tile, tile), tile)
-        lane_of = lax.broadcasted_iota(jnp.int32, (pivot_count, total), 1)
-        row_of = lax.broadcasted_iota(jnp.int32, (pivot_count, total), 0) + start
+    def solve(round_index, inverse, span):
+        rows = slice(round_index * pivot_count, (round_index + 1) * pivot_count)
+        slot = round_index % 2
+        values = product(inverse, (rest_high[slot, :, span], rest_low[slot, :, span]))
+        held[rows, span] = values
+        if round_index + 1 < rounds:
+            done_high[rows, span], done_low[rows, span] = split_two(values)
+
+    def copy_out(round_index):
+        rows = slice(round_index * pivot_count, (round_index + 1) * pivot_count)
+        return pltpu.make_async_copy(held.at[rows], out_ref.at[rows], sems.at[round_index])
+
+    inverse_parts = None
+    for round_index in range(rounds):
+        start = round_index * pivot_count
+        end = start + pivot_count
         own = covariance(
-            start, pivot_count, [anchors_ref[axis:axis + 1, :] for axis in range(dims)]
+            start, [anchors_ref[axis:axis + 1, start:] for axis in range(dims)]
         )
-        own = own + jnp.where(row_of == lane_of, nugget_level, 0.0)
-        table[here, :] = jnp.where(lane_of >= start, own, 0.0)
-
-        def subtract(earlier, inner):
-            before = pl.multiple_of(earlier * pivot_count, pivot_count)
-            seen = pl.ds(before, pivot_count)
-            kept = (lane_of < before + pivot_count) | (lane_of >= start)
-            table[here, :] = table[here, :] - lax.dot_general(
-                table[seen, here],
-                jnp.where(kept, table[seen, :], 0.0),
-                (((0,), (0,)), ((), ())),
+        shape = own.shape
+        own = own + jnp.where(
+            lax.broadcasted_iota(jnp.int32, shape, 0)
+            == lax.broadcasted_iota(jnp.int32, shape, 1),
+            nugget_level,
+            0.0,
+        )
+        lower_parts = None
+        if round_index:
+            lower = jnp.transpose(table[:start, start:end])
+            own = own - jnp.dot(
+                lower,
+                table[:start, start:],
                 precision=HIGHEST,
                 preferred_element_type=jnp.float32,
             )
-            return inner
-
-        lax.fori_loop(0, round_index, subtract, 0)
-
-        targets = [
-            points_ref[axis:axis + 1, span]
-            * jnp.concatenate([weights[axis]] * (tile // LANES), axis=1)
-            for axis in range(dims)
-        ]
+            lower_parts = split_two(lower)
 
         def beside(step, steps):
-            size = total // steps
-            part = slice(step * size, (step + 1) * size)
-            values = covariance(step * size, size, targets)
-            high = values.astype(jnp.bfloat16)
-            block_high[part, span] = high
-            block_low[part, span] = (values - high.astype(jnp.float32)).astype(jnp.bfloat16)
-
-        inverse = invert_factor(table[here, here], beside)
-        table[here, :] = jnp.dot(
-            inverse, table[here, :], precision=HIGHEST, preferred_element_type=jnp.float32
-        )
-        table[here, here] = inverse
-        final = jnp.where(lane_of < start + pivot_count, table[here, :], 0.0)
-        high = final.astype(jnp.bfloat16)
-        inverse_high[here, :] = high
-        inverse_low[here, :] = (final - high.astype(jnp.float32)).astype(jnp.bfloat16)
-        return carry
-
-    lax.fori_loop(0, rounds, one_round, 0)
-
-    half = total // 2
-
-    def copy_out(index):
-        span = pl.ds(pl.multiple_of(index * tile, tile), tile)
-        return pltpu.make_async_copy(held.at[:, span], out_ref.at[:, span], sems.at[index])
-
-    def product(rows, depth, span):
-        def multiply(a, b):
-            return jnp.dot(
-                a[rows, depth], b[depth, span], preferred_element_type=jnp.float32
+            width = point_count // steps
+            ready = (step + 1) * width
+            if ready % chunk:
+                return
+            for low in range(max(0, ready - max(width, chunk)), ready, chunk):
+                span = slice(low, low + chunk)
+                if round_index:
+                    solve(round_index - 1, inverse_parts, span)
+                targets = [
+                    points_ref[axis:axis + 1, span]
+                    * jnp.concatenate([weights[axis]] * (chunk // LANES), axis=1)
+                    for axis in range(dims)
+                ]
+                rest = covariance(start, targets)
+                if round_index:
+                    rest = rest - product(
+                        lower_parts, (done_high[:start, span], done_low[:start, span])
+                    )
+                slot = round_index % 2
+                rest_high[slot, :, span], rest_low[slot, :, span] = split_two(rest)
+
+        inverse = invert_factor(own[:, :pivot_count], beside)
+        if round_index:
+            copy_out(round_index - 1).start()
+        if round_index + 1 < rounds:
+            table[start:end, end:] = jnp.dot(
+                inverse,
+                own[:, pivot_count:],
+                precision=HIGHEST,
+                preferred_element_type=jnp.float32,
             )
-
-        return (
-            multiply(inverse_high, block_low) + multiply(inverse_low, block_high)
-        ) + multiply(inverse_high, block_high)
-
-    def one_tile(index, carry):
-        span = pl.ds(pl.multiple_of(index * tile, tile), tile)
-        top, bottom = slice(0, half), slice(half, total)
-        held[:, span] = product(slice(0, total), top, span)
-        held[bottom, span] = held[bottom, span] + product(bottom, bottom, span)
-        copy_out(index).start()
-        return carry
-
-    lax.fori_loop(0, rounds, one_tile, 0)
-
-    def finish(index, carry):
-        copy_out(index).wait()
-        return carry
-
-    lax.fori_loop(0, rounds, finish, 0)
+        inverse_parts = split_two(inverse)
+
+    solve(rounds - 1, inverse_parts, slice(0, point_count))
+    copy_out(rounds - 1).start()
+    for round_index in range(rounds):
+        copy_out(round_index).wait()
 
 
 def per_device(mesh_shape, points, scales, pivots):
@@ -399,8 +402,8 @@
             pltpu.VMEM((dims, point_count), jnp.float32),
             pltpu.VMEM((total, total), jnp.float32),
             pltpu.VMEM((dims, total, LANES), jnp.float32),
-            pltpu.VMEM((total, total), jnp.bfloat16),
-            pltpu.VMEM((total, total), jnp.bfloat16),
+            pltpu.VMEM((2, pivot_count, point_count), jnp.bfloat16),
+            pltpu.VMEM((2, pivot_count, point_count), jnp.bfloat16),
             pltpu.VMEM((total, point_count), jnp.bfloat16),
             pltpu.VMEM((total, point_count), jnp.bfloat16),
             pltpu.VMEM((total, point_count), jnp.float32),

time: 39 us -> 32.2 us (0.83)
  Pallas kernels: 38.7 us -> 31.8 us
    pallas_call x1, Pallas kernels: 26 us -> 19.1 us  [per_device(): pl.pallas_call(functools.partial(factor_kernel, rounds), out_shape=jax.Sh...]
where the time goes in v3:
time: 32.2 us; the launch traced here: 31.9 us
  Pallas kernels  31.8 us (99%)
    pallas_call x1, Pallas kernels, per_device(): pl.pallas_call(functools.partial(factor_kernel, rounds), out_shape=jax.Sh...  19.1 us
    pallas_call x1, Pallas kernels, per_device(): pl.pallas_call(functools.partial(exchange_kernel, mesh_shape, inner), out...  12.7 us

profile of v3, /device:TPU:0, one launch (start us, length us, event | category | flops | bytes accessed | tf_op | source)
XLA Modules:
  0.0 31.9 jit_solution(15302286968864839582)
XLA Ops:
  0.0 12.7 %exchange_anchors.1.anchors_ref = f32[8,512]{1,0:T(8,128)} custom-call(f32[3,2048]{1,0:T(4,128)} %points_hbm.3, f32[3]{0:T(128)} %scales_hbm.1, s32[4,128]{1,0:T(4,128)} %pivots_hbm.1), custom_call_target="tpu_custom_call" | custom-call | tf_op jit(solution)/shard_map/exchange_anchors/pallas_call | solution.py:371
  12.7 19.1 %factor_columns.1 = f32[512,2048]{1,0:T(8,128)} custom-call(f32[3,2048]{1,0:T(4,128)} %points_hbm.3, f32[8,512]{1,0:T(8,128)} %exchange_anchors.1.anchors_ref), custom_call_target="tpu_custom_call" | custom-call | tf_op jit(solution)/shard_map/factor_columns/pallas_call | solution.py:396

commit v4 on v3

--- a/solution.py
+++ b/solution.py
@@ -29,6 +29,7 @@
     scales_hbm,
     pivots_hbm,
     out_ref,
+    scaled_ref,
     points_ref,
     scales_ref,
     pivots_ref,
@@ -97,6 +98,14 @@
             )
         mine[:, round_index * pivot_count:(round_index + 1) * pivot_count] = total[:dims]
 
+    constant = math.sqrt(0.5 * math.log2(math.e))
+    weights = [
+        constant / jnp.full((1, LANES), scales_ref[axis], jnp.float32) for axis in range(dims)
+    ]
+    for axis in range(dims):
+        scaled_ref[axis:axis + 1, :] = points_ref[axis:axis + 1, :] * jnp.concatenate(
+            [weights[axis]] * chunks, axis=1
+        )
     pl.semaphore_wait(barrier, len(near) + len(far))
 
     def exchange(source, landed, targets, send_sems, recv_sems):
@@ -122,12 +131,11 @@
     total, near_copies = exchange(mine, landed_near, near, near_send, near_recv)
     pair_sum[...] = total
     total, far_copies = exchange(pair_sum, landed_far, far, far_send, far_recv)
-    constant = math.sqrt(0.5 * math.log2(math.e))
     out_ref[...] = jnp.zeros_like(out_ref)
     for axis in range(dims):
-        weight = constant / jnp.full((1, total.shape[1]), scales_ref[axis], jnp.float32)
-        out_ref[axis:axis + 1, :] = total[axis:axis + 1, :] * weight
-        out_ref[dims + axis:dims + axis + 1, :] = weight
+        out_ref[axis:axis + 1, :] = total[axis:axis + 1, :] * jnp.concatenate(
+            [weights[axis]] * (total.shape[1] // LANES), axis=1
+        )
     for copy in near_copies + far_copies:
         copy.wait_send()
 
@@ -239,10 +247,9 @@
 
 def factor_kernel(
     rounds,
-    points_hbm,
+    points_ref,
     anchors_ref,
     out_ref,
-    points_ref,
     table,
     anchor_wide,
     rest_high,
@@ -250,20 +257,16 @@
     done_high,
     done_low,
     held,
-    load_sem,
     sems,
+    last_sems,
 ):
     dims, point_count = points_ref.shape
     total = anchors_ref.shape[1]
     pivot_count = total // rounds
     chunk = 2 * LANES
-    load = pltpu.make_async_copy(points_hbm, points_ref, load_sem)
-    load.start()
-    weights = [anchors_ref[dims + axis:dims + axis + 1, :LANES] for axis in range(dims)]
     upright = jnp.transpose(anchors_ref[...])
     for axis in range(dims):
         anchor_wide[axis] = jnp.broadcast_to(upright[:, axis:axis + 1], (total, LANES))
-    load.wait()
 
     def covariance(start, targets):
         pieces = []
@@ -324,11 +327,7 @@
                 span = slice(low, low + chunk)
                 if round_index:
                     solve(round_index - 1, inverse_parts, span)
-                targets = [
-                    points_ref[axis:axis + 1, span]
-                    * jnp.concatenate([weights[axis]] * (chunk // LANES), axis=1)
-                    for axis in range(dims)
-                ]
+                targets = [points_ref[axis:axis + 1, span] for axis in range(dims)]
                 rest = covariance(start, targets)
                 if round_index:
                     rest = rest - product(
@@ -349,10 +348,22 @@
             )
         inverse_parts = split_two(inverse)
 
-    solve(rounds - 1, inverse_parts, slice(0, point_count))
-    copy_out(rounds - 1).start()
-    for round_index in range(rounds):
+    last_rows = slice(total - pivot_count, total)
+    width = point_count // rounds
+    last_copies = []
+    for piece in range(rounds):
+        span = slice(piece * width, (piece + 1) * width)
+        solve(rounds - 1, inverse_parts, span)
+        last_copies.append(
+            pltpu.make_async_copy(
+                held.at[last_rows, span], out_ref.at[last_rows, span], last_sems.at[piece]
+            )
+        )
+        last_copies[-1].start()
+    for round_index in range(rounds - 1):
         copy_out(round_index).wait()
+    for copy in last_copies:
+        copy.wait()
 
 
 def per_device(mesh_shape, points, scales, pivots):
@@ -368,11 +379,14 @@
     near, far = inner - 1, devices // inner - 1
     vmem = pl.BlockSpec(memory_space=pltpu.VMEM)
     anywhere = pl.BlockSpec(memory_space=pl.ANY)
-    anchors = pl.pallas_call(
+    anchors, scaled = pl.pallas_call(
         functools.partial(exchange_kernel, mesh_shape, inner),
-        out_shape=jax.ShapeDtypeStruct((GROUP, total), jnp.float32),
+        out_shape=[
+            jax.ShapeDtypeStruct((GROUP, total), jnp.float32),
+            jax.ShapeDtypeStruct((dims, point_count), jnp.float32),
+        ],
         in_specs=[anywhere] * 3,
-        out_specs=vmem,
+        out_specs=[vmem, vmem],
         scratch_shapes=[
             pltpu.VMEM((dims, point_count), jnp.float32),
             pltpu.SMEM((dims,), jnp.float32),
@@ -396,10 +410,9 @@
     return pl.pallas_call(
         functools.partial(factor_kernel, rounds),
         out_shape=jax.ShapeDtypeStruct((total, point_count), jnp.float32),
-        in_specs=[anywhere, vmem],
+        in_specs=[vmem, vmem],
         out_specs=anywhere,
         scratch_shapes=[
-            pltpu.VMEM((dims, point_count), jnp.float32),
             pltpu.VMEM((total, total), jnp.float32),
             pltpu.VMEM((dims, total, LANES), jnp.float32),
             pltpu.VMEM((2, pivot_count, point_count), jnp.bfloat16),
@@ -407,12 +420,12 @@
             pltpu.VMEM((total, point_count), jnp.bfloat16),
             pltpu.VMEM((total, point_count), jnp.bfloat16),
             pltpu.VMEM((total, point_count), jnp.float32),
-            pltpu.SemaphoreType.DMA,
+            pltpu.SemaphoreType.DMA((rounds,)),
             pltpu.SemaphoreType.DMA((rounds,)),
         ],
         compiler_params=pltpu.CompilerParams(vmem_limit_bytes=56 * 2 ** 20),
         name="factor_columns",
-    )(points, anchors)
+    )(scaled, anchors)
 
 
 def solution(mesh):

time: 32.2 us -> 31.4 us (0.975)
  Pallas kernels: 31.8 us -> 31 us
    pallas_call x1, Pallas kernels: 19.1 us -> 18.3 us  [per_device(): pl.pallas_call(functools.partial(factor_kernel, rounds), out_shape=jax.Sh...]
where the time goes in v4:
time: 31.4 us; the launch traced here: 31.2 us
  Pallas kernels  31 us (99%)
    pallas_call x1, Pallas kernels, per_device(): pl.pallas_call(functools.partial(factor_kernel, rounds), out_shape=jax.Sh...  18.3 us
    pallas_call x1, Pallas kernels, per_device(): pl.pallas_call(functools.partial(exchange_kernel, mesh_shape, inner), out...  12.7 us

profile of v4, /device:TPU:0, one launch (start us, length us, event | category | flops | bytes accessed | tf_op | source)
XLA Modules:
  0.0 31.2 jit_solution(2737533913313464696)
XLA Ops:
  0.0 12.7 %exchange_anchors.1 = (f32[8,512]{1,0:T(8,128)}, f32[3,2048]{1,0:T(4,128)}) custom-call(f32[3,2048]{1,0:T(4,128)} %points_hbm.1, f32[3]{0:T(128)} %scales_hbm.1, s32[4,128]{1,0:T(4,128)} %pivots_hbm.1), custom_call_target="tpu_custom_call" | custom-call | tf_op jit(solution)/shard_map/exchange_anchors/pallas_call | solution.py:382
  12.7 18.3 %factor_columns.1 = f32[512,2048]{1,0:T(8,128)} custom-call(f32[3,2048]{1,0:T(4,128)} %get-tuple-element.7.points_ref, f32[8,512]{1,0:T(8,128)} %get-tuple-element.8.anchors_ref), custom_call_target="tpu_custom_call" | custom-call | tf_op jit(solution)/shard_map/factor_columns/pallas_call | solution.py:410
